TPU v7x, 512 devices: a whole 4x4x16 slice. The times are simulated.
512 devices in a mesh: seq: 64 (over x, z), mp: 4 (over y), dp: 2 (over core).
Axes of the slice: x: 4, y: 4, z: 16, core: 2. Of those that a mesh axis runs over, the one named last changes fastest.
Arguments:
- queries: bfloat16 [2, 128, 64, 2048], P('dp', 'seq', None, 'mp'), may hold values from -6 to 6
- out_grad: bfloat16 [2, 128, 64, 2048], P('dp', 'seq', None, 'mp'), may hold values from -6 to 6
- encoded: bfloat16 [2, 256, 128, 896], P('dp', None, 'seq', 'mp'), may hold values from -6 to 6
- key_weight: bfloat16 [896, 2048], P(None, 'mp'), may hold values from -0.1875 to 0.1875
- value_weight: bfloat16 [896, 2048], P(None, 'mp'), may hold values from -0.1875 to 0.1875
- neighbour_ids: int32 [2, 128, 2], P('dp'), may hold values from 0 to 255
- neighbour_counts: int32 [2, 128], P('dp', 'seq'), may hold values from 1 to 2
Outputs:
- attended: bfloat16 [2, 128, 64, 2048], P('dp', 'seq', None, 'mp')
- query_grad: bfloat16 [2, 128, 64, 2048], P('dp', 'seq', None, 'mp')
- key_weight_grad: bfloat16 [896, 2048], P(None, ('mp', 'dp'))
- value_weight_grad: bfloat16 [896, 2048], P(None, ('mp', 'dp'))
All inputs are finite; a program needn't handle non-finite values.
Results may differ from a plain program's by a relative error of at most 0.017.
Values may be sent and summed in bfloat16 or wider, within the bound.
A program may use at most 64 MiB of HBM per device.

v0:
```python
import jax
import jax.numpy as jnp
from jax import lax
from jax.sharding import PartitionSpec as P

HD = 128


def contract_rows(left, right):
    return lax.dot_general(
        left, right, (((0,), (0,)), ((), ())), preferred_element_type=jnp.float32
    )


def body(queries, out_grad, encoded, key_weight, value_weight, neighbour_ids, neighbour_counts):
    block_count = queries.shape[1]
    block_len = queries.shape[2]
    features = queries.shape[3]
    heads = features // HD
    pairs = neighbour_ids.shape[2]
    needs = block_count * pairs
    scale = HD ** (-0.5)
    weights = jnp.concatenate([key_weight, value_weight], axis=1)
    local_rows = encoded[0]
    outgoing = local_rows[neighbour_ids[0].reshape(-1)]
    slot_rows = lax.all_to_all(outgoing, "seq", split_axis=0, concat_axis=1, tiled=True)
    span = slot_rows.shape[1]
    full_rows = lax.all_gather(slot_rows, "mp", axis=2, tiled=True).reshape(needs * span, -1)
    slot_kv = jnp.dot(full_rows, weights, preferred_element_type=jnp.float32).astype(jnp.bfloat16)
    slot_kv = slot_kv.reshape(block_count, pairs * span, 2 * features)
    keys = slot_kv[:, :, :features].reshape(block_count, pairs * span, heads, HD)
    values = slot_kv[:, :, features:].reshape(block_count, pairs * span, heads, HD)
    query = queries[0].reshape(block_count, block_len, heads, HD)
    grad_out = out_grad[0].reshape(block_count, block_len, heads, HD)
    slot_of_key = jnp.arange(pairs * span, dtype=jnp.int32) // span
    valid = slot_of_key[None, :] < neighbour_counts[0][:, None]
    scores = jnp.einsum("cqhd,ckhd->chqk", query, keys, preferred_element_type=jnp.float32) * scale
    scores = jnp.where(valid[:, None, None, :], scores, -1e30)
    top = jnp.max(scores, axis=-1, keepdims=True)
    expo = jnp.exp(scores - top)
    probs = expo / jnp.sum(expo, axis=-1, keepdims=True)
    probs_low = probs.astype(jnp.bfloat16)
    heads_out = jnp.einsum("chqk,ckhd->cqhd", probs_low, values, preferred_element_type=jnp.float32)
    attended = heads_out.astype(jnp.bfloat16).reshape(1, block_count, block_len, features)
    grad_probs = jnp.einsum("cqhd,ckhd->chqk", grad_out, values, preferred_element_type=jnp.float32)
    delta = jnp.einsum("cqhd,cqhd->chq", grad_out.astype(jnp.float32), heads_out)
    grad_scores = probs * (grad_probs - delta[..., None])
    grad_low = grad_scores.astype(jnp.bfloat16)
    query_grad = (
        jnp.einsum("chqk,ckhd->cqhd", grad_low, keys, preferred_element_type=jnp.float32) * scale
    )
    query_grad = query_grad.astype(jnp.bfloat16).reshape(1, block_count, block_len, features)
    key_grad = (
        jnp.einsum("chqk,cqhd->ckhd", grad_low, query, preferred_element_type=jnp.float32) * scale
    ).astype(jnp.bfloat16)
    value_grad = jnp.einsum(
        "chqk,cqhd->ckhd", probs_low, grad_out, preferred_element_type=jnp.float32
    ).astype(jnp.bfloat16)
    slot_grad = jnp.concatenate(
        [key_grad.reshape(-1, features), value_grad.reshape(-1, features)], axis=1
    )
    weight_grad = contract_rows(full_rows, slot_grad)
    grad_keys = weight_grad[:, :features]
    grad_values = weight_grad[:, features:]
    summed = lax.psum((grad_keys, grad_values), "seq")
    shares = (
        lax.psum_scatter(
            summed[0].astype(jnp.bfloat16), "dp", scatter_dimension=1, tiled=True
        ).astype(jnp.float32),
        lax.psum_scatter(
            summed[1].astype(jnp.bfloat16), "dp", scatter_dimension=1, tiled=True
        ).astype(jnp.float32),
    )
    return (attended, query_grad, shares[0].astype(jnp.bfloat16), shares[1].astype(jnp.bfloat16))


def solution(mesh):
    return jax.shard_map(
        body,
        mesh=mesh,
        in_specs=(
            P("dp", "seq", None, "mp"),
            P("dp", "seq", None, "mp"),
            P("dp", None, "seq", "mp"),
            P(None, "mp"),
            P(None, "mp"),
            P("dp", None, None),
            P("dp", "seq"),
        ),
        out_specs=(
            P("dp", "seq", None, "mp"),
            P("dp", "seq", None, "mp"),
            P(None, ("mp", "dp")),
            P(None, ("mp", "dp")),
        ),
        check_vma=False,
    )
```

profile of v0, /device:TPU:1, one launch (start us, length us, event | category | flops | bytes accessed | tf_op | source)
XLA Modules:
  0.0 442.2 jit_solution(4475389134396412508)
XLA Ops:
  7.2 0.0 copy-start.1
  7.2 0.8 copy.51
  8.0 0.1 reshape_squeeze.9
  8.1 1.1 copy.50
  9.3 1.9 gather_fusion
  11.2 19.1 %all-to-all-start = ((bf16[256,2,224]{2,1,0:T(2,128)(2,1)}), bf16[256,2,224]{2,1,0:T(2,128)(2,1)S(1)}, u32[]{:S(2)}, u32[]{:S(2)}) async-start(bf16[256,2,224]{2,1,0:T(2,128)(2,1)} %gather_fusion), calls=%async_computation | async-start | bytes 524288 | tf_op jit(solution)/shard_map/all_to_all | solution.py:26
  30.3 0.0 reduce-scatter.3.cloned.1.call-start
  30.3 0.9 reshape_squeeze.11
  31.3 0.9 reshape_squeeze.10
  32.2 0.0 copy-done.1
  32.2 0.1 broadcast_compare_fusion
  32.3 17.0 %all-to-all-done = bf16[256,2,224]{2,1,0:T(2,128)(2,1)S(1)} async-done(((bf16[256,2,224]{2,1,0:T(2,128)(2,1)}), bf16[256,2,224]{2,1,0:T(2,128)(2,1)S(1)}, u32[]{:S(2)}, u32[]{:S(2)}) %all-to-all-start) | async-done | bytes 229408 | tf_op jit(solution)/shard_map/all_to_all | solution.py:26
  49.3 0.1 copy.52
  49.5 0.2 copy.53
  49.7 11.9 %all_gather.3 = bf16[4,128,896]{1,0,2:T(4,128)(2,1)S(1)} all-gather(bf16[4,128,224]{1,0,2:T(4,128)(2,1)S(1)} %copy.53), channel_id=1, replica_groups=mesh['seq'=64,'mp'=4,'dp'=2] {'mp'}, dimensions={2}, use_global_device_ids=true | all-gather | bytes 1146880 | tf_op jit(solution)/shard_map/all_gather | solution.py:28
  61.6 1.1 copy.54
  62.7 2.7 fusion.5
  65.4 0.1 fusion.35
  65.5 0.2 copy.81
  65.7 0.2 copy.80
  65.9 0.2 fusion.16
  66.1 1.4 fusion.36
  67.5 1.6 bitcast_convert_fusion
  69.2 2.1 fusion.11
  71.2 1.4 copy.68
  72.7 0.9 multiply_reduce_fusion
  73.6 0.9 copy.78
  74.5 0.2 fusion.17
  74.8 0.3 fusion.12
  75.1 0.4 copy.66
  75.5 0.1 copy_bitcast_fusion
  75.7 1.2 fusion.20
  76.8 1.6 fusion.34
  78.5 0.0 copy-start
  78.5 268.8 %all-reduce.2 = (bf16[896,512]{1,0:T(8,128)(2,1)}, bf16[896,512]{1,0:T(8,128)(2,1)}) all-reduce(f32[896,512]{1,0:T(8,128)} %get-tuple-element.7, f32[896,512]{1,0:T(8,128)S(1)} %get-tuple-element.6), channel_id=1, replica_groups=mesh['seq'=64,'mp'=4,'dp'=2] {'seq'}, use_global_device_ids=true, to_apply=%region_2.3 | all-reduce | flops 917504 | bytes 5505024 | tf_op jit(solution)/shard_map/psum | solution.py:65
  347.3 0.0 reduce-scatter.3.cloned.1.call-update
  347.3 0.0 reduce-scatter.5.cloned.1.call-start
  347.3 0.7 reduce-scatter.5.cloned.1.call-update
  348.0 0.0 copy-done
  348.0 0.1 copy.60
  348.2 0.7 reshape.106
  348.9 0.3 fusion.19
  349.2 0.1 copy.64
  349.3 0.7 reshape.107
  350.0 61.6 %reduce-scatter.3.cloned.1.call-done = bf16[896,256]{1,0:T(8,128)(2,1)} async-done(((bf16[896,512]{1,0:T(8,128)(2,1)}), bf16[896,256]{1,0:T(8,128)(2,1)}) %reduce-scatter.3.cloned.1.call-update) | async-done | bytes 458768 | tf_op jit(solution)/shard_map/reduce_scatter | solution.py:67
  411.6 23.8 %reduce-scatter.5.cloned.1.call-done = bf16[896,256]{1,0:T(8,128)(2,1)} async-done(((bf16[896,512]{1,0:T(8,128)(2,1)}), bf16[896,256]{1,0:T(8,128)(2,1)}) %reduce-scatter.5.cloned.1.call-update) | async-done | bytes 458768 | tf_op jit(solution)/shard_map/reduce_scatter | solution.py:70
  (3 shorter events, 0.0 us)
Async XLA Ops:
  7.2 25.1 %copy-start.1 = (s32[1,2]{1,0:T(1,128)S(1)}, s32[1,2]{1,0:T(1,128)}, u32[]{:S(2)}) copy-start(s32[1,2]{1,0:T(1,128)} %param.13) | copy-start | bytes 28
  11.2 38.2 %all-to-all-start = ((bf16[256,2,224]{2,1,0:T(2,128)(2,1)}), bf16[256,2,224]{2,1,0:T(2,128)(2,1)S(1)}, u32[]{:S(2)}, u32[]{:S(2)}) async-start(bf16[256,2,224]{2,1,0:T(2,128)(2,1)} %gather_fusion), calls=%async_computation | async-start | bytes 524288 | tf_op jit(solution)/shard_map/all_to_all | solution.py:26
  30.3 381.3 %reduce-scatter.3.cloned.1.call-start = ((), (), s32[]{:S(2)}) async-start(), calls=%async_computation.3 | async-start | bytes 1376256 | tf_op jit(solution)/shard_map/reduce_scatter | solution.py:67
  78.5 269.6 %copy-start = (bf16[2,64,4,128]{3,1,2,0:T(8,128)(2,1)S(1)}, bf16[2,64,4,128]{3,1,2,0:T(8,128)(2,1)}, u32[]{:S(2)}) copy-start(bf16[2,64,4,128]{3,1,2,0:T(8,128)(2,1)} %get-tuple-element.12) | copy-start | bytes 393220
  347.3 88.1 %reduce-scatter.5.cloned.1.call-start = ((), (), s32[]{:S(2)}) async-start(), calls=%async_computation.4 | async-start | bytes 1376256 | tf_op jit(solution)/shard_map/reduce_scatter | solution.py:70
Sparse Core Ops, SparseCore 0:
  347.4 64.1 reduce-scatter.2
  415.2 20.1 reduce-scatter.4
where the time goes:
time: 443 us; the launch traced here: 442 us
  blocking collectives  281 us (63%)
  waiting for transfers between devices  103 us (23%)
  starting transfers between devices  19.2 us (4%)
  between operations  14.2 us (3%)
  local copies, waits for them, and re-layouts  14 us (3%)
  matrix products  8.69 us (2%)
    psum x1, blocking collectives, body(): summed = lax.psum((grad_keys, grad_values), 'seq')  269 us
    reduce_scatter x1, waiting for transfers between devices, body(): lax.psum_scatter(summed[0].astype(jnp.bfloat16), 'dp', scatter_dimension=...  61.6 us
    reduce_scatter x1, waiting for transfers between devices, body(): lax.psum_scatter(summed[1].astype(jnp.bfloat16), 'dp', scatter_dimension=...  23.8 us
    all_to_all x1, starting transfers between devices, body(): lax.all_to_all(outgoing, 'seq', split_axis=0, concat_axis=1, tiled=True)  19.1 us
    all_to_all x1, waiting for transfers between devices, body(): lax.all_to_all(outgoing, 'seq', split_axis=0, concat_axis=1, tiled=True)  17 us
    all_gather x1, blocking collectives, body(): lax.all_gather(slot_rows, 'mp', axis=2, tiled=True)  11.9 us
  transfers between devices with their start and end apart: 3, of which 3 were waited for; matrix products, arithmetic and copies ran while one was open for 1% of the time, Pallas kernels for 0%

commit v1 on v0

v1 whole, which is shorter than its diff:
```python
import functools

import jax
import jax.numpy as jnp
from jax import lax
from jax.experimental import pallas as pl
from jax.experimental.pallas import tpu as pltpu
from jax.sharding import PartitionSpec as P

HD = 128
NX, NZ, NM = 4, 16, 4
MESH = pl.DeviceIdType.MESH
BF = jnp.bfloat16
F32 = jnp.float32
SHIFT = [0] + [(p + 1) // 2 if p % 2 else NZ - p // 2 for p in range(1, NZ)]


def dot(a, b, dims):
    return lax.dot_general(a, b, ((dims[:1], dims[1:]), ((), ())), preferred_element_type=F32)


def wait_bytes(ref, sem):
    pltpu.make_async_copy(ref, ref, sem).wait()


def kernel(
    idx_ref, counts_ref, enc_ref, q_hbm, og_hbm, wk_hbm, wv_hbm,
    att_ref, qg_ref, wg_ref,
    w, q, og, outgoing, zbuf, rows, rows_t, kv, sg, dps, dpr, hf, xs, xr, zf, zs, zr,
    load_sem, send_sem, az_sem, ax_sem, ay_sem, dp_sem, rx_sem, rz_sem, gz_sem, gx_sem,
):
    seq = lax.axis_index("seq")
    m = lax.axis_index("mp")
    d = lax.axis_index("dp")
    x, z = seq // NZ, lax.rem(seq, NZ)
    ze, zj = lax.rem(z, 4), z // 4

    def along_z(k):
        return {"seq": x * NZ + lax.rem(z + k, NZ)}

    def along_x(k):
        return {"seq": lax.rem(x + k, NX) * NZ + z}

    def along_m(k):
        return {"mp": lax.rem(m + k, NM)}

    sibling = {"dp": 1 - d}

    def send(src, dst, phase, recv, device):
        pltpu.make_async_remote_copy(
            src_ref=src, dst_ref=dst, send_sem=send_sem.at[phase], recv_sem=recv,
            device_id=device, device_id_type=MESH,
        ).start()

    barrier = pltpu.get_barrier_semaphore()
    peers = [along_z(k) for k in range(1, NZ)] + [along_x(k) for k in range(1, NX)]
    peers += [along_m(k) for k in range(1, NM)] + [sibling]
    for peer in peers:
        pl.semaphore_signal(barrier, inc=1, device_id=peer, device_id_type=MESH)

    loads = []
    for e in range(NM):
        for half, hbm in enumerate((wk_hbm, wv_hbm)):
            loads.append(pltpu.make_async_copy(
                hbm.at[pl.ds(224 * e, 224)],
                w.at[pl.ds(256 * e, 224), pl.ds(512 * half, 512)],
                load_sem.at[len(loads)],
            ))
    loads.append(pltpu.make_async_copy(q_hbm, q, load_sem.at[8]))
    loads.append(pltpu.make_async_copy(og_hbm, og, load_sem.at[9]))
    for load in loads:
        load.start()
    for e in range(NM):
        w[pl.ds(256 * e + 224, 32), :] = jnp.zeros((32, 1024), BF)

    place = lax.broadcasted_iota(jnp.int32, (512, 512), 0)
    chosen = jnp.where(place == idx_ref[...], 1.0, 0.0).astype(BF)
    outgoing[...] = dot(chosen, enc_ref[...], (0, 0)).astype(BF).reshape(NZ, NX, 8, 256)
    zbuf[0] = outgoing[z]

    pl.semaphore_wait(barrier, len(peers))

    for p in range(1, NZ):
        send(outgoing.at[lax.rem(z + SHIFT[p], NZ)], zbuf.at[p], 0, az_sem.at[p // 4], along_z(SHIFT[p]))
    mine = pl.ds(pl.multiple_of(m * 256, 256), 256)

    def to_x(g):
        low = max(4 * g, 1)
        wait_bytes(zbuf.at[pl.ds(low, 4 * g + 4 - low)], az_sem.at[g])
        for s in range(1, NX):
            send(zbuf.at[pl.ds(4 * g, 4), lax.rem(x + s, NX)], rows.at[g, s, :, :, mine], 1, ax_sem.at[g], along_x(s))
        rows[g, 0, :, :, mine] = zbuf[pl.ds(4 * g, 4), x]

    def to_m(g):
        wait_bytes(rows.at[g, pl.ds(1, 3), :, :, mine], ax_sem.at[g])
        for t in range(1, NM):
            send(rows.at[g, :, :, :, mine], rows.at[g, :, :, :, mine], 2, ay_sem.at[g], along_m(t))

    to_x(0)
    for g in range(1, 4):
        to_x(g)
        to_m(g - 1)
    to_m(3)
    for load in loads:
        load.wait()
    for g in range(4):
        wait_bytes(rows.at[g, :, :, :, pl.ds(0, 768)], ay_sem.at[g])

    flat = rows[...].reshape(512, 1024)
    for c in range(4):
        cols = pl.ds(256 * c, 256)
        kv[:, cols] = dot(flat, w[:, cols], (1, 0)).astype(BF)
    rows_t[...] = flat.T

    scale = HD ** (-0.5)
    key = lax.broadcasted_iota(jnp.int32, (128, 512), 1)
    owner = lax.broadcasted_iota(jnp.int32, (128, 512), 0) // 64
    count = jnp.where(owner == 0, counts_ref[0, 0], counts_ref[0, 1])
    valid = (((key // 2) & 1) == owner) & ((key & 1) < count)
    for h in range(4):
        cols = pl.ds(HD * h, HD)
        vcols = pl.ds(512 + HD * h, HD)
        qh, gh, kh, vh = q[:, cols], og[:, cols], kv[:, cols], kv[:, vcols]
        scores = jnp.where(valid, dot(qh, kh, (1, 1)) * scale, -1e30)
        expo = jnp.exp(scores - jnp.max(scores, axis=-1, keepdims=True))
        probs = expo * (1.0 / jnp.sum(expo, axis=-1, keepdims=True))
        low = probs.astype(BF)
        heads = dot(low, vh, (1, 0))
        att_ref[:, cols] = heads.astype(BF)
        delta = jnp.sum(gh.astype(F32) * heads, axis=-1, keepdims=True)
        grad = (probs * (dot(gh, vh, (1, 1)) - delta)).astype(BF)
        qg_ref[:, cols] = (dot(grad, kh, (1, 0)) * scale).astype(BF)
        sg[:, cols] = (dot(grad, qh, (0, 0)) * scale).astype(BF)
        sg[:, vcols] = dot(low, gh, (0, 0)).astype(BF)

    def partial(e, side, half):
        cols = pl.ds(pl.multiple_of(512 * half + 256 * side, 256), 256)
        return dot(rows_t[pl.ds(256 * e, 256), :], sg[:, cols], (1, 0))[:224]

    for e in range(4):
        for half in range(2):
            part = partial(e, 1 - d, half)
            for c in range(2):
                dps[e, 2 * half + c] = part[:, 128 * c:128 * c + 128].reshape(4, 56, 128).astype(BF)
        send(dps.at[e], dpr.at[e], 3, dp_sem.at[e], sibling)
    for e in range(4):
        parts = [partial(e, d, half) for half in range(2)]
        wait_bytes(dpr.at[e], dp_sem.at[e])
        for half in range(2):
            for c in range(2):
                tile = 2 * half + c
                both = parts[half][:, 128 * c:128 * c + 128].reshape(4, 56, 128) + dpr[e, tile].astype(F32)
                hf[tile, e] = both
                xs[tile, e] = both.astype(BF)
        for s in range(1, NX):
            send(xs.at[lax.rem(x + s, NX), e], xr.at[s - 1, e], 4, rx_sem.at[e], along_x(s))
    for e in range(4):
        wait_bytes(xr.at[:, e], rx_sem.at[e])
        total = hf[x, e] + xr[0, e].astype(F32) + xr[1, e].astype(F32) + xr[2, e].astype(F32)
        zf[e] = total
        zs[e] = total.astype(BF)
        for i in range(4):
            j = lax.rem(zj + i, 4)
            ahead = lax.rem(4 * j + e - z + NZ, NZ)

            def go():
                send(zs.at[e, j], zr.at[15 - ahead], 5, rz_sem.at[0], along_z(ahead))

            if i == 0:
                pl.when(ze != e)(go)
            else:
                go()
    wait_bytes(zr, rz_sem.at[0])
    total = zf[ze, zj]
    for k in range(NZ - 1):
        total += zr[k].astype(F32)
    own = 4 * ze + zj
    wg_ref[x, own] = total.astype(BF)
    for k in range(1, NZ):
        send(wg_ref.at[x, own], wg_ref.at[x, own], 6, gz_sem.at[ze], along_z(SHIFT[k]))
    for e in range(4):
        @pl.when(ze == e)
        def _():
            wait_bytes(zr.at[pl.ds(0, 3)], gz_sem.at[e])

        @pl.when(ze != e)
        def _():
            wait_bytes(zr.at[pl.ds(0, 4)], gz_sem.at[e])

        for s in range(1, NX):
            block = wg_ref.at[x, pl.ds(4 * e, 4)]
            send(block, block, 7, gx_sem.at[0], along_x(s))
    wait_bytes(xr, gx_sem.at[0])

    wait_bytes(zbuf.at[pl.ds(1, 15)], send_sem.at[0])
    wait_bytes(zbuf.at[pl.ds(0, 12)], send_sem.at[1])
    wait_bytes(rows.at[:, :, :, :, pl.ds(0, 768)], send_sem.at[2])
    wait_bytes(dps, send_sem.at[3])
    wait_bytes(xr, send_sem.at[4])
    wait_bytes(zr, send_sem.at[5])
    wait_bytes(zr, send_sem.at[6])
    wait_bytes(xr, send_sem.at[7])


def body(queries, out_grad, encoded, key_weight, value_weight, neighbour_ids, neighbour_counts):
    enc = jnp.pad(encoded[0].reshape(512, 224), ((0, 0), (0, 32)))
    ids = neighbour_ids[0].reshape(NX, NZ, 1, 4).transpose(1, 0, 2, 3)
    token = jnp.arange(2, dtype=jnp.int32).reshape(1, 1, 2, 1)
    idx = (2 * ids + token).reshape(1, 512)
    vmem = pl.BlockSpec(memory_space=pltpu.VMEM)
    hbm = pl.BlockSpec(memory_space=pl.ANY)
    dma = pltpu.SemaphoreType.DMA
    att, qg, wg = pl.pallas_call(
        kernel,
        out_shape=(
            jax.ShapeDtypeStruct((128, 512), BF),
            jax.ShapeDtypeStruct((128, 512), BF),
            jax.ShapeDtypeStruct((4, 16, 56, 128), BF),
        ),
        in_specs=[vmem, pl.BlockSpec(memory_space=pltpu.SMEM), vmem, hbm, hbm, hbm, hbm],
        out_specs=(vmem, vmem, vmem),
        scratch_shapes=[
            pltpu.VMEM((1024, 1024), BF),
            pltpu.VMEM((128, 512), BF),
            pltpu.VMEM((128, 512), BF),
            pltpu.VMEM((NZ, NX, 8, 256), BF),
            pltpu.VMEM((NZ, NX, 8, 256), BF),
            pltpu.VMEM((4, NX, 4, 8, 1024), BF),
            pltpu.VMEM((1024, 512), BF),
            pltpu.VMEM((512, 1024), BF),
            pltpu.VMEM((512, 1024), BF),
            pltpu.VMEM((4, 4, 4, 56, 128), BF),
            pltpu.VMEM((4, 4, 4, 56, 128), BF),
            pltpu.VMEM((4, 4, 4, 56, 128), F32),
            pltpu.VMEM((4, 4, 4, 56, 128), BF),
            pltpu.VMEM((3, 4, 4, 56, 128), BF),
            pltpu.VMEM((4, 4, 56, 128), F32),
            pltpu.VMEM((4, 4, 56, 128), BF),
            pltpu.VMEM((15, 56, 128), BF),
            dma((10,)), dma((8,)), dma((4,)), dma((4,)), dma((4,)),
            dma((4,)), dma((4,)), dma((1,)), dma((4,)), dma((1,)),
        ],
        compiler_params=pltpu.CompilerParams(
            collective_id=0, has_side_effects=True, vmem_limit_bytes=56 * 1024 * 1024
        ),
        cost_estimate=pl.CostEstimate(flops=2_500_000_000, bytes_accessed=4_000_000, transcendentals=262144),
    )(
        idx, neighbour_counts, enc,
        queries.reshape(128, 512), out_grad.reshape(128, 512), key_weight, value_weight,
    )
    grads = wg.reshape(4, 896, 128)
    kwg = jnp.concatenate([grads[0], grads[1]], axis=1)
    vwg = jnp.concatenate([grads[2], grads[3]], axis=1)
    return att.reshape(1, 2, 64, 512), qg.reshape(1, 2, 64, 512), kwg, vwg


def solution(mesh):
    return jax.shard_map(
        body,
        mesh=mesh,
        in_specs=(
            P("dp", "seq", None, "mp"),
            P("dp", "seq", None, "mp"),
            P("dp", None, "seq", "mp"),
            P(None, "mp"),
            P(None, "mp"),
            P("dp", None, None),
            P("dp", "seq"),
        ),
        out_specs=(
            P("dp", "seq", None, "mp"),
            P("dp", "seq", None, "mp"),
            P(None, ("mp", "dp")),
            P(None, ("mp", "dp")),
        ),
        check_vma=False,
    )
```

time: 443 us -> 101 us (0.23)
  the two profiles are of different devices: /device:TPU:1 before, /device:TPU:32 now
where the time goes in v1:
time: 101 us
  Pallas kernels  93.3 us (92%)
  local copies, waits for them, and re-layouts  5.05 us (5%)
  other arithmetic  1.77 us (2%)
    pallas_call x1, Pallas kernels, body(): pl.pallas_call(kernel, out_shape=(jax.ShapeDtypeStruct((128, 512), BF), j...  93.3 us

profile of v1, /device:TPU:32, one launch (start us, length us, event | category | flops | bytes accessed | tf_op | source)
XLA Modules:
  0.0 100.8 jit_solution(4255799839883966374)
XLA Ops:
  0.6 0.0 copy-start
  0.6 0.7 broadcast_multiply_fusion
  1.4 0.1 copy.12
  1.5 0.1 mul.15
  1.6 0.7 add.31.idx_ref
  2.3 0.0 copy-done
  2.3 0.2 copy.14
  2.5 0.2 reshape_squeeze.4
  2.8 0.7 pad.4.enc_ref
  3.5 93.3 %shard_map.102 = (bf16[128,512]{1,0:T(8,128)(2,1)}, bf16[128,512]{1,0:T(8,128)(2,1)}, bf16[4,16,56,128]{3,2,1,0:T(8,128)(2,1)}) custom-call(s32[1,512]{1,0:T(1,128)} %add.31.idx_ref, s32[1,2]{1,0:T(1,128)} %counts_ref.1, bf16[512,256]{1,0:T(8,128)(2,1)} %pad.4.enc_ref, bf16[128,512]{1,0:T(8,128)(2,1)} %bitcast.18, bf16[128,512]{1,0:T(8,128)(2,1)} %bitcast.19, ...), custom_call_target="tpu_custom_call" | custom-call | flops 2500000000 | bytes 4000000 | tf_op jit(solution)/shard_map/pallas_call | solution.py:213
  96.8 1.4 %fusion = (bf16[1,16,56,128]{3,2,1,0:T(8,128)(2,1)S(1)}, bf16[1,16,56,128]{3,2,1,0:T(8,128)(2,1)S(1)}, bf16[1,16,56,128]{3,2,1,0:T(8,128)(2,1)S(1)}, bf16[1,16,56,128]{3,2,1,0:T(8,128)(2,1)S(1)}) fusion(bf16[4,16,56,128]{3,2,1,0:T(8,128)(2,1)} %get-tuple-element.9), kind=kLoop, calls=%fused_computation.4 | loop fusion | bytes 1835008 | tf_op jit(solution)/shard_map/slice | solution.py:253
  98.2 0.0 copy-start.2
  98.2 1.0 %pad_maximum_fusion = (bf16[896,256]{1,0:T(8,128)(2,1)}, bf16[896,256]{1,0:T(8,128)(2,1)}) fusion(bf16[896,128]{1,0:T(8,128)(2,1)S(1)} %bitcast.13, bf16[896,128]{1,0:T(8,128)(2,1)S(1)} %bitcast.14, bf16[896,128]{1,0:T(8,128)(2,1)S(1)} %bitcast.12, bf16[896,128]{1,0:T(8,128)(2,1)S(1)} %bitcast.11), kind=kLoop, calls=%fused_computation | loop fusion | flops 1835008 | bytes 1835008 | tf_op jit(solution)/shard_map/concatenate | solution.py:252
  99.2 0.0 copy-done.2
  99.2 0.0 copy-start.1
  99.2 0.7 copy.17
  99.9 0.3 copy-done.1
  100.2 0.7 copy.18
  (2 shorter events, 0.0 us)
Async XLA Ops:
  0.6 1.7 %copy-start = (bf16[1,256,2,224]{1,3,2,0:T(8,128)(2,1)S(1)}, bf16[1,256,2,224]{1,3,2,0:T(8,128)(2,1)}, u32[]{:S(2)}) copy-start(bf16[1,256,2,224]{1,3,2,0:T(8,128)(2,1)} %param.9) | copy-start | bytes 688132
  98.2 1.0 %copy-start.2 = (bf16[128,512]{1,0:T(8,128)(2,1)S(1)}, bf16[128,512]{1,0:T(8,128)(2,1)}, u32[]{:S(2)}) copy-start(bf16[128,512]{1,0:T(8,128)(2,1)} %get-tuple-element.7) | copy-start | bytes 393220
  99.2 1.0 copy-start.1

commit v2 on v1

v2 whole, which is shorter than its diff:
```python
import functools

import jax
import jax.numpy as jnp
from jax import lax
from jax.experimental import pallas as pl
from jax.experimental.pallas import tpu as pltpu
from jax.sharding import PartitionSpec as P

HD = 128
NX, NZ, NM = 4, 16, 4
MESH = pl.DeviceIdType.MESH
BF = jnp.bfloat16
F32 = jnp.float32
SHIFT = [0] + [(p + 1) // 2 if p % 2 else NZ - p // 2 for p in range(1, NZ)]


def dot(a, b, dims):
    return lax.dot_general(a, b, ((dims[:1], dims[1:]), ((), ())), preferred_element_type=F32)


def wait_bytes(ref, sem):
    pltpu.make_async_copy(ref, ref, sem).wait()


GROUPS = ((0, 6), (6, 11), (11, 14), (14, 16))
RA, RB = 32, 24


def kernel(
    ids_ref, counts_ref, enc_ref, q_hbm, og_hbm, wk_hbm, wv_hbm,
    att_hbm, qg_hbm, ga, gb,
    w, q, og, att, qg, outgoing, zbuf, rows, rows_t, kv, sg, dps, dpr,
    ha, hb, xsa, zsb, xra, znb, zfa, zsa, zna, hbx, xsb, xrb, ffa, fsa, fra, ffb, fsb, frb,
    load_sem, send_sem, az_sem, ax_sem, ay_sem, dp_sem, rxa_sem, one_sem, gna_sem,
):
    seq = lax.axis_index("seq")
    m = lax.axis_index("mp")
    d = lax.axis_index("dp")
    x, z = seq // NZ, lax.rem(seq, NZ)
    ze, zj = lax.rem(z, 4), z // 4

    def along_z(k):
        return {"seq": x * NZ + lax.rem(z + (k + NZ) % NZ, NZ)}

    def along_x(k):
        return {"seq": lax.rem(x + k, NX) * NZ + z}

    def along_m(k):
        return {"mp": lax.rem(m + k, NM)}

    sibling = {"dp": 1 - d}

    def send(src, dst, phase, recv, device):
        pltpu.make_async_remote_copy(
            src_ref=src, dst_ref=dst, send_sem=send_sem.at[phase], recv_sem=recv,
            device_id=device, device_id_type=MESH,
        ).start()

    barrier = pltpu.get_barrier_semaphore()
    peers = [along_z(k) for k in range(1, NZ)] + [along_x(k) for k in range(1, NX)]
    peers += [along_m(k) for k in range(1, NM)] + [sibling]
    for peer in peers:
        pl.semaphore_signal(barrier, inc=1, device_id=peer, device_id_type=MESH)

    loads = []
    for e in range(NM):
        for half, hbm in enumerate((wk_hbm, wv_hbm)):
            loads.append(pltpu.make_async_copy(
                hbm.at[pl.ds(224 * e, 224)],
                w.at[pl.ds(256 * e, 224), pl.ds(512 * half, 512)],
                load_sem.at[len(loads)],
            ))
    loads.append(pltpu.make_async_copy(q_hbm, q, load_sem.at[8]))
    loads.append(pltpu.make_async_copy(og_hbm, og, load_sem.at[9]))
    for load in loads:
        load.start()

    lane = lax.broadcasted_iota(jnp.int32, (128, 512), 1)
    part = lax.broadcasted_iota(jnp.int32, (128, 512), 0)
    stretch = ((lane // 8) % NX) * (2 * NZ) + (lane // 32) * 2 + (lane // 2) % 2
    wanted = jnp.zeros((8, 512), F32)
    for slot in range(2):
        pick = jnp.where((part == stretch) & (lane % 2 == slot), 1.0, 0.0).astype(BF)
        ids = jnp.broadcast_to(ids_ref[pl.ds(slot, 1), :], (8, 128)).astype(F32).astype(BF)
        wanted += dot(ids, pick, (1, 0))
    wanted = wanted[:1].astype(jnp.int32)
    place = lax.broadcasted_iota(jnp.int32, (256, 512), 0)
    token = (lax.broadcasted_iota(jnp.int32, (1, 512), 1) // 4) % 2
    found = jnp.zeros((224, 512), F32)
    for t in range(2):
        chosen = jnp.where(place == jnp.where(token == t, wanted, -1), 1.0, 0.0).astype(BF)
        found += dot(enc_ref[t], chosen, (1, 0))
    found = jnp.concatenate([found, jnp.zeros((32, 512), F32)], axis=0)
    outgoing[...] = found.T.astype(BF).reshape(NZ, NX, 8, 256)
    zbuf[0] = outgoing[z]

    pl.semaphore_wait(barrier, len(peers))

    group_of = [g for g, (low, high) in enumerate(GROUPS) for _ in range(low, high)]
    for p in range(1, NZ):
        send(outgoing.at[lax.rem(z + SHIFT[p], NZ)], zbuf.at[p], 0, az_sem.at[group_of[p]], along_z(SHIFT[p]))
    for e in range(NM):
        w[pl.ds(256 * e + 224, 32), :] = jnp.zeros((32, 1024), BF)
    mine = pl.ds(pl.multiple_of(m * 256, 256), 256)

    def to_x(g):
        low, high = GROUPS[g]
        some = pl.ds(low, high - low)
        first = max(low, 1)
        wait_bytes(zbuf.at[pl.ds(first, high - first)], az_sem.at[g])
        for s in range(1, NX):
            send(zbuf.at[some, lax.rem(x + s, NX)], rows.at[some, s, :, mine], 1, ax_sem.at[g], along_x(s))
        rows[some, 0, :, mine] = zbuf[some, x]

    def to_m(g):
        low, high = GROUPS[g]
        some = pl.ds(low, high - low)
        wait_bytes(rows.at[some, pl.ds(1, 3), :, mine], ax_sem.at[g])
        for t in range(1, NM):
            send(rows.at[some, :, :, mine], rows.at[some, :, :, mine], 2, ay_sem.at[g], along_m(t))

    to_x(0)
    for g in range(1, len(GROUPS)):
        to_x(g)
        to_m(g - 1)
    to_m(len(GROUPS) - 1)
    for load in loads:
        load.wait()
    for g, (low, high) in enumerate(GROUPS):
        wait_bytes(rows.at[pl.ds(low, high - low), :, :, pl.ds(0, 768)], ay_sem.at[g])

    flat = rows[...].reshape(512, 1024)
    for c in range(4):
        cols = pl.ds(256 * c, 256)
        kv[:, cols] = dot(flat, w[:, cols], (1, 0)).astype(BF)
    rows_t[...] = flat.T

    scale = HD ** (-0.5)
    key = lax.broadcasted_iota(jnp.int32, (128, 512), 1)
    owner = lax.broadcasted_iota(jnp.int32, (128, 512), 0) // 64
    count = jnp.where(owner == 0, counts_ref[0, 0], counts_ref[0, 1])
    valid = (((key // 2) & 1) == owner) & ((key & 1) < count)
    for h in range(4):
        cols = pl.ds(HD * h, HD)
        vcols = pl.ds(512 + HD * h, HD)
        qh, gh, kh, vh = q[:, cols], og[:, cols], kv[:, cols], kv[:, vcols]
        scores = jnp.where(valid, dot(qh, kh, (1, 1)) * scale, -1e30)
        expo = jnp.exp(scores - jnp.max(scores, axis=-1, keepdims=True))
        probs = expo * (1.0 / jnp.sum(expo, axis=-1, keepdims=True))
        low = probs.astype(BF)
        heads = dot(low, vh, (1, 0))
        att[:, cols] = heads.astype(BF)
        delta = jnp.sum(gh.astype(F32) * heads, axis=-1, keepdims=True)
        grad = (probs * (dot(gh, vh, (1, 1)) - delta)).astype(BF)
        qg[:, cols] = (dot(grad, kh, (1, 0)) * scale).astype(BF)
        sg[:, cols] = (dot(grad, qh, (0, 0)) * scale).astype(BF)
        sg[:, vcols] = dot(low, gh, (0, 0)).astype(BF)
    stores = [
        pltpu.make_async_copy(att, att_hbm, load_sem.at[0]),
        pltpu.make_async_copy(qg, qg_hbm, load_sem.at[1]),
    ]
    for store in stores:
        store.start()

    def partial(e, side, half):
        cols = pl.ds(pl.multiple_of(512 * half + 256 * side, 256), 256)
        return dot(rows_t[pl.ds(256 * e, 256), :], sg[:, cols], (1, 0))[:224]

    def to_class(k, whole, first, second, src, dst, phase, sem):
        @pl.when(k == 1)
        def _():
            send(src(whole), dst(0, whole), phase, sem, along_z(1))

        @pl.when(k == 3)
        def _():
            send(src(whole), dst(1, whole), phase, sem, along_z(-1))

        @pl.when(k == 2)
        def _():
            send(src(first), dst(2, first), phase, sem, along_z(2))
            send(src(second), dst(2, second), phase, sem, along_z(-2))

    whole, first, second = pl.ds(0, 4), pl.ds(0, 2), pl.ds(2, 2)
    for e in range(4):
        for half in range(2):
            part = partial(e, 1 - d, half)
            for c in range(2):
                dps[e, 2 * half + c] = part[:, 128 * c:128 * c + 128].reshape(4, 56, 128).astype(BF)
        send(dps.at[e], dpr.at[e], 3, dp_sem.at[e], sibling)
    for e in range(4):
        parts = [partial(e, d, half) for half in range(2)]
        wait_bytes(dpr.at[e], dp_sem.at[e])
        for half in range(2):
            for c in range(2):
                tile = 2 * half + c
                both = parts[half][:, 128 * c:128 * c + 128].reshape(4, 56, 128) + dpr[e, tile].astype(F32)
                ha[tile, e], hb[e, tile] = both[:, :RA], both[:, RA:]
                xsa[tile, e], zsb[e, tile] = both[:, :RA].astype(BF), both[:, RA:].astype(BF)
        for s in range(1, NX):
            send(xsa.at[lax.rem(x + s, NX), e], xra.at[s - 1, e], 4, rxa_sem.at[e], along_x(s))
        to_class(
            lax.rem(e - ze + 4, 4), whole, first, second,
            lambda some: zsb.at[e, some], lambda slot, some: znb.at[slot, some], 5, one_sem.at[0],
        )

    def add(base, received, *where):
        for s in range(3):
            base += received[(s, *where)].astype(F32)
        return base

    def fold_a(e):
        wait_bytes(xra.at[:, e], rxa_sem.at[e])
        total = add(ha[x, e], xra, e)
        zfa[e] = total
        zsa[e] = total.astype(BF)
        to_class(
            lax.rem(e - ze + 4, 4), whole, first, second,
            lambda some: zsa.at[e, some], lambda slot, some: zna.at[slot, some], 6, one_sem.at[1],
        )

    fold_a(0)
    fold_a(1)
    wait_bytes(znb, one_sem.at[0])
    for tile in range(4):
        total = add(hb[ze, tile], znb, tile)
        hbx[tile] = total
        xsb[tile] = total.astype(BF)
    for s in range(1, NX):
        send(xsb.at[lax.rem(x + s, NX)], xrb.at[s - 1], 7, one_sem.at[2], along_x(s))
    fold_a(2)
    fold_a(3)
    wait_bytes(xrb, one_sem.at[2])
    total = add(hbx[x], xrb)
    ffb[...] = total
    fsb[...] = total.astype(BF)
    for i in range(1, 4):
        send(fsb.at[lax.rem(zj + i, 4)], frb.at[i - 1], 9, one_sem.at[4], along_z(4 * i))
    wait_bytes(zna, one_sem.at[1])
    total = add(zfa[ze], zna)
    ffa[...] = total
    fsa[...] = total.astype(BF)
    for i in range(1, 4):
        send(fsa.at[lax.rem(zj + i, 4)], fra.at[i - 1], 8, one_sem.at[3], along_z(4 * i))
    wait_bytes(frb, one_sem.at[4])
    gb[ze, x, zj] = add(ffb[zj], frb).astype(BF)
    for i in range(1, 4):
        send(gb.at[ze, x, zj], gb.at[ze, x, zj], 11, one_sem.at[6], along_z(4 * i))
    wait_bytes(fra, one_sem.at[3])
    ga[x, ze, zj] = add(ffa[zj], fra).astype(BF)
    for i in range(1, 4):
        send(ga.at[x, ze, zj], ga.at[x, ze, zj], 10, one_sem.at[5], along_z(4 * i))

    wait_bytes(frb, one_sem.at[6])
    for s in range(1, NX):
        send(gb.at[ze, x], gb.at[ze, x], 14, one_sem.at[8], along_x(s))
    wait_bytes(fra, one_sem.at[5])
    for i, (shift, some) in enumerate(((1, whole), (-1, whole), (2, first), (-2, second))):
        send(ga.at[x, ze, some], ga.at[x, ze, some], 12, gna_sem.at[min(i, 2)], along_z(shift))
    for s in range(1, NX):
        send(ga.at[x, ze], ga.at[x, ze], 13, one_sem.at[7], along_x(s))
    wait_bytes(xrb, one_sem.at[8])
    for shift, some in ((1, whole), (-1, whole), (2, first), (-2, second)):
        send(gb.at[ze, some], gb.at[ze, some], 15, one_sem.at[9], along_z(shift))
    for i, k in enumerate((3, 1, 2)):
        wait_bytes(zna.at[i], gna_sem.at[i])
        group = lax.rem(ze + k, 4)
        for s in range(1, NX):
            send(ga.at[x, group], ga.at[x, group], 13, one_sem.at[7], along_x(s))
    wait_bytes(znb, one_sem.at[9])
    wait_bytes(xra, one_sem.at[7])

    for store in stores:
        store.wait()
    wait_bytes(zbuf.at[pl.ds(1, 15)], send_sem.at[0])
    wait_bytes(rows.at[:, pl.ds(1, 3), :, pl.ds(0, 256)], send_sem.at[1])
    wait_bytes(rows.at[:, :, :, pl.ds(0, 768)], send_sem.at[2])
    for phase, sized in enumerate((dps, xra, znb, zna, xrb, fra, frb, fra, frb, zna, xra, xrb, znb)):
        wait_bytes(sized, send_sem.at[phase + 3])


def place(att_in, qg_in, ga, gb, att_out, qg_out, kg_out, vg_out):
    att_out[...] = att_in[...]
    qg_out[...] = qg_in[...]
    for tile in range(4):
        out = (kg_out, vg_out)[tile // 2]
        lanes = pl.ds(128 * (tile % 2), 128)
        out[:, :, pl.ds(0, RA), lanes] = ga[tile]
        out[:, :, pl.ds(RA, RB), lanes] = gb[:, tile]


def body(queries, out_grad, encoded, key_weight, value_weight, neighbour_ids, neighbour_counts):
    vmem = pl.BlockSpec(memory_space=pltpu.VMEM)
    hbm = pl.BlockSpec(memory_space=pl.ANY)
    dma = pltpu.SemaphoreType.DMA

    def bf(*shape):
        return pltpu.VMEM(shape, BF)

    def f32(*shape):
        return pltpu.VMEM(shape, F32)

    low = jax.ShapeDtypeStruct((128, 512), BF)
    att, qg, ga, gb = pl.pallas_call(
        kernel,
        out_shape=(
            low, low,
            jax.ShapeDtypeStruct((4, 4, 4, RA, 128), BF),
            jax.ShapeDtypeStruct((4, 4, 4, RB, 128), BF),
        ),
        in_specs=[vmem, pl.BlockSpec(memory_space=pltpu.SMEM), vmem, hbm, hbm, hbm, hbm],
        out_specs=(hbm, hbm, vmem, vmem),
        scratch_shapes=[
            bf(1024, 1024), bf(128, 512), bf(128, 512), bf(128, 512), bf(128, 512),
            bf(NZ, NX, 8, 256), bf(NZ, NX, 8, 256),
            bf(NZ, NX, 8, 1024), bf(1024, 512), bf(512, 1024), bf(512, 1024),
            bf(4, 4, 4, 56, 128), bf(4, 4, 4, 56, 128),
            f32(4, 4, 4, RA, 128), f32(4, 4, 4, RB, 128),
            bf(4, 4, 4, RA, 128), bf(4, 4, 4, RB, 128),
            bf(3, 4, 4, RA, 128), bf(3, 4, 4, RB, 128),
            f32(4, 4, RA, 128), bf(4, 4, RA, 128), bf(3, 4, RA, 128),
            f32(4, 4, RB, 128), bf(4, 4, RB, 128), bf(3, 4, RB, 128),
            f32(4, RA, 128), bf(4, RA, 128), bf(3, RA, 128),
            f32(4, RB, 128), bf(4, RB, 128), bf(3, RB, 128),
            dma((10,)), dma((16,)), dma((4,)), dma((4,)), dma((4,)),
            dma((4,)), dma((4,)), dma((10,)), dma((3,)),
        ],
        compiler_params=pltpu.CompilerParams(
            collective_id=0, has_side_effects=True, vmem_limit_bytes=56 * 1024 * 1024
        ),
        cost_estimate=pl.CostEstimate(flops=2_500_000_000, bytes_accessed=4_000_000, transcendentals=262144),
    )(
        neighbour_ids[0].T, neighbour_counts, encoded[0].transpose(1, 2, 0),
        queries.reshape(128, 512), out_grad.reshape(128, 512), key_weight, value_weight,
    )
    grad = jax.ShapeDtypeStruct((4, 4, 56, 256), BF)
    att, qg, kg, vg = pl.pallas_call(
        place,
        out_shape=(low, low, grad, grad),
        in_specs=[vmem] * 4,
        out_specs=(vmem,) * 4,
    )(att, qg, ga, gb)
    return (
        att.reshape(1, 2, 64, 512), qg.reshape(1, 2, 64, 512),
        kg.reshape(896, 256), vg.reshape(896, 256),
    )


def solution(mesh):
    return jax.shard_map(
        body,
        mesh=mesh,
        in_specs=(
            P("dp", "seq", None, "mp"),
            P("dp", "seq", None, "mp"),
            P("dp", None, "seq", "mp"),
            P(None, "mp"),
            P(None, "mp"),
            P("dp", None, None),
            P("dp", "seq"),
        ),
        out_specs=(
            P("dp", "seq", None, "mp"),
            P("dp", "seq", None, "mp"),
            P(None, ("mp", "dp")),
            P(None, ("mp", "dp")),
        ),
        check_vma=False,
    )
```

time: 101 us -> 86.9 us (0.86)
  Pallas kernels: 93.3 us -> 86.1 us
  local copies, waits for them, and re-layouts: 5.05 us -> 0 us
  other arithmetic: 1.77 us -> 0 us
    pallas_call x1 -> x2, Pallas kernels: 93.3 us -> 86.1 us  [the longest x1 83.7 us: body(): pl.pallas_call(kernel, out_shape=(low, low, jax.ShapeDtypeStruct((4, 4, 4...]
    unnamed x9 -> x0, local copies, waits for them, and re-layouts: 1.79 us -> none
    slice x1 -> x0, local copies, waits for them, and re-layouts: 1.36 us -> none  [body(): vwg = jnp.concatenate([grads[2], grads[3]], axis=1)]
    concatenate x1 -> x0, other arithmetic: 1.02 us -> none  [body(): kwg = jnp.concatenate([grads[0], grads[1]], axis=1)]
where the time goes in v2:
time: 86.9 us; the launch traced here: 86.7 us
  Pallas kernels  86.1 us (99%)
    pallas_call x1, Pallas kernels, body(): pl.pallas_call(kernel, out_shape=(low, low, jax.ShapeDtypeStruct((4, 4, 4...  83.7 us
    pallas_call x1, Pallas kernels, body(): pl.pallas_call(place, out_shape=(low, low, grad, grad), in_specs=[vmem] *...  2.43 us

profile of v2, /device:TPU:32, one launch (start us, length us, event | category | flops | bytes accessed | tf_op | source)
XLA Modules:
  0.0 86.7 jit_solution(18364143950181694901)
XLA Ops:
  0.6 83.7 %shard_map.102 = (bf16[128,512]{1,0:T(8,128)(2,1)}, bf16[128,512]{1,0:T(8,128)(2,1)}, bf16[4,4,4,32,128]{4,3,2,1,0:T(8,128)(2,1)}, bf16[4,4,4,24,128]{4,3,2,1,0:T(8,128)(2,1)}) custom-call(s32[2,128]{1,0:T(2,128)} %bitcast.19, s32[1,2]{1,0:T(1,128)} %counts_ref.1, bf16[2,224,256]{2,1,0:T(8,128)(2,1)} %bitcast.14, bf16[128,512]{1,0:T(8,128)(2,1)} %bitcast.15, ...), custom_call_target="tpu_custom_call" | custom-call | flops 2500000000 | bytes 4000000 | tf_op jit(solution)/shard_map/pallas_call | solution.py:304
  84.3 2.4 %shard_map.103 = (bf16[128,512]{1,0:T(8,128)(2,1)}, bf16[128,512]{1,0:T(8,128)(2,1)}, bf16[4,4,56,256]{3,2,1,0:T(8,128)(2,1)}, bf16[4,4,56,256]{3,2,1,0:T(8,128)(2,1)}) custom-call(bf16[128,512]{1,0:T(8,128)(2,1)} %get-tuple-element.12.att_in, bf16[128,512]{1,0:T(8,128)(2,1)} %get-tuple-element.13.qg_in, bf16[4,4,4,32,128]{4,3,2,1,0:T(8,128)(2,1)} %get-tuple-element.14.ga, ...), custom_call_target="tpu_custom_call" | custom-call | tf_op jit(solution)/shard_map/pallas_call | solution.py:337

commit v3 on v2

--- a/solution.py
+++ b/solution.py
@@ -12,7 +12,8 @@
 MESH = pl.DeviceIdType.MESH
 BF = jnp.bfloat16
 F32 = jnp.float32
-SHIFT = [0] + [(p + 1) // 2 if p % 2 else NZ - p // 2 for p in range(1, NZ)]
+SHIFT = (0, 8, 7, 9, 6, 10, 5, 11, 4, 12, 3, 13, 2, 14, 1, 15)
+OTHERS = (2, 1, 3)
 
 
 def dot(a, b, dims):
@@ -23,16 +24,16 @@
     pltpu.make_async_copy(ref, ref, sem).wait()
 
 
-GROUPS = ((0, 6), (6, 11), (11, 14), (14, 16))
+FROM_X = (0, 1, 3, 2)
 RA, RB = 32, 24
 
 
 def kernel(
     ids_ref, counts_ref, enc_ref, q_hbm, og_hbm, wk_hbm, wv_hbm,
     att_hbm, qg_hbm, ga, gb,
-    w, q, og, att, qg, outgoing, zbuf, rows, rows_t, kv, sg, dps, dpr,
+    w, q, og, att, qg, outgoing, held, rows, rows_t, kv, sg, dps, dpr,
     ha, hb, xsa, zsb, xra, znb, zfa, zsa, zna, hbx, xsb, xrb, ffa, fsa, fra, ffb, fsb, frb,
-    load_sem, send_sem, az_sem, ax_sem, ay_sem, dp_sem, rxa_sem, one_sem, gna_sem,
+    load_sem, send_sem, ax_sem, az_sem, ay_sem, dp_sem, rxa_sem, one_sem, gna_sem,
 ):
     seq = lax.axis_index("seq")
     m = lax.axis_index("mp")
@@ -41,7 +42,7 @@
     ze, zj = lax.rem(z, 4), z // 4
 
     def along_z(k):
-        return {"seq": x * NZ + lax.rem(z + (k + NZ) % NZ, NZ)}
+        return {"seq": x * NZ + lax.rem(z + k + NZ, NZ)}
 
     def along_x(k):
         return {"seq": lax.rem(x + k, NX) * NZ + z}
@@ -78,7 +79,7 @@
 
     lane = lax.broadcasted_iota(jnp.int32, (128, 512), 1)
     part = lax.broadcasted_iota(jnp.int32, (128, 512), 0)
-    stretch = ((lane // 8) % NX) * (2 * NZ) + (lane // 32) * 2 + (lane // 2) % 2
+    stretch = (lane // 8) * 2 + (lane // 2) % 2
     wanted = jnp.zeros((8, 512), F32)
     for slot in range(2):
         pick = jnp.where((part == stretch) & (lane % 2 == slot), 1.0, 0.0).astype(BF)
@@ -92,70 +93,78 @@
         chosen = jnp.where(place == jnp.where(token == t, wanted, -1), 1.0, 0.0).astype(BF)
         found += dot(enc_ref[t], chosen, (1, 0))
     found = jnp.concatenate([found, jnp.zeros((32, 512), F32)], axis=0)
-    outgoing[...] = found.T.astype(BF).reshape(NZ, NX, 8, 256)
-    zbuf[0] = outgoing[z]
+    outgoing[...] = found.T.astype(BF).reshape(NX, NZ, 8, 256)
+    held[0] = outgoing[x]
 
     pl.semaphore_wait(barrier, len(peers))
 
-    group_of = [g for g, (low, high) in enumerate(GROUPS) for _ in range(low, high)]
-    for p in range(1, NZ):
-        send(outgoing.at[lax.rem(z + SHIFT[p], NZ)], zbuf.at[p], 0, az_sem.at[group_of[p]], along_z(SHIFT[p]))
+    for i in (3, 1, 2):
+        send(outgoing.at[lax.rem(x + FROM_X[i], NX)], held.at[i], 0, ax_sem.at[i], along_x(FROM_X[i]))
+    mine = pl.ds(pl.multiple_of(m * 256, 256), 256)
+
+    def to_z(i):
+        if i > 0:
+            wait_bytes(held.at[i], ax_sem.at[i])
+        for p in range(1, NZ):
+            send(held.at[i, lax.rem(z + SHIFT[p], NZ)], rows.at[i, p, :, mine], 1, az_sem.at[i], along_z(SHIFT[p]))
+        rows[i, 0, :, mine] = held[i, z]
+
+    def to_m(i):
+        wait_bytes(rows.at[i, pl.ds(1, NZ - 1), :, mine], az_sem.at[i])
+        for t in OTHERS:
+            send(rows.at[i, :, :, mine], rows.at[i, :, :, mine], 2, ay_sem.at[i], along_m(t))
+
+    def project(low, high):
+        for i in range(low, high):
+            wait_bytes(rows.at[i, :, :, pl.ds(0, 768)], ay_sem.at[i])
+        some = pl.ds(128 * low, 128 * (high - low))
+        flat = rows[pl.ds(low, high - low)].reshape(128 * (high - low), 1024)
+        for c in range(4):
+            cols = pl.ds(256 * c, 256)
+            kv[some, cols] = dot(flat, w[:, cols], (1, 0)).astype(BF)
+        rows_t[:, some] = flat.T
+
+    to_z(0)
+    to_z(1)
+    to_z(2)
     for e in range(NM):
         w[pl.ds(256 * e + 224, 32), :] = jnp.zeros((32, 1024), BF)
-    mine = pl.ds(pl.multiple_of(m * 256, 256), 256)
-
-    def to_x(g):
-        low, high = GROUPS[g]
-        some = pl.ds(low, high - low)
-        first = max(low, 1)
-        wait_bytes(zbuf.at[pl.ds(first, high - first)], az_sem.at[g])
-        for s in range(1, NX):
-            send(zbuf.at[some, lax.rem(x + s, NX)], rows.at[some, s, :, mine], 1, ax_sem.at[g], along_x(s))
-        rows[some, 0, :, mine] = zbuf[some, x]
-
-    def to_m(g):
-        low, high = GROUPS[g]
-        some = pl.ds(low, high - low)
-        wait_bytes(rows.at[some, pl.ds(1, 3), :, mine], ax_sem.at[g])
-        for t in range(1, NM):
-            send(rows.at[some, :, :, mine], rows.at[some, :, :, mine], 2, ay_sem.at[g], along_m(t))
-
-    to_x(0)
-    for g in range(1, len(GROUPS)):
-        to_x(g)
-        to_m(g - 1)
-    to_m(len(GROUPS) - 1)
+    to_m(0)
+    to_z(3)
     for load in loads:
         load.wait()
-    for g, (low, high) in enumerate(GROUPS):
-        wait_bytes(rows.at[pl.ds(low, high - low), :, :, pl.ds(0, 768)], ay_sem.at[g])
-
-    flat = rows[...].reshape(512, 1024)
-    for c in range(4):
-        cols = pl.ds(256 * c, 256)
-        kv[:, cols] = dot(flat, w[:, cols], (1, 0)).astype(BF)
-    rows_t[...] = flat.T
+    for i in range(1, NX):
+        to_m(i)
+    project(0, 3)
+    project(3, 4)
 
     scale = HD ** (-0.5)
     key = lax.broadcasted_iota(jnp.int32, (128, 512), 1)
     owner = lax.broadcasted_iota(jnp.int32, (128, 512), 0) // 64
     count = jnp.where(owner == 0, counts_ref[0, 0], counts_ref[0, 1])
     valid = (((key // 2) & 1) == owner) & ((key & 1) < count)
-    for h in range(4):
-        cols = pl.ds(HD * h, HD)
-        vcols = pl.ds(512 + HD * h, HD)
-        qh, gh, kh, vh = q[:, cols], og[:, cols], kv[:, cols], kv[:, vcols]
-        scores = jnp.where(valid, dot(qh, kh, (1, 1)) * scale, -1e30)
-        expo = jnp.exp(scores - jnp.max(scores, axis=-1, keepdims=True))
-        probs = expo * (1.0 / jnp.sum(expo, axis=-1, keepdims=True))
-        low = probs.astype(BF)
-        heads = dot(low, vh, (1, 0))
-        att[:, cols] = heads.astype(BF)
-        delta = jnp.sum(gh.astype(F32) * heads, axis=-1, keepdims=True)
-        grad = (probs * (dot(gh, vh, (1, 1)) - delta)).astype(BF)
-        qg[:, cols] = (dot(grad, kh, (1, 0)) * scale).astype(BF)
-        sg[:, cols] = (dot(grad, qh, (0, 0)) * scale).astype(BF)
-        sg[:, vcols] = dot(low, gh, (0, 0)).astype(BF)
+    heads = range(4)
+    cols = [pl.ds(HD * h, HD) for h in heads]
+    vcols = [pl.ds(512 + HD * h, HD) for h in heads]
+    qs, gs = [q[:, c] for c in cols], [og[:, c] for c in cols]
+    ks, vs = [kv[:, c] for c in cols], [kv[:, c] for c in vcols]
+    scores = [jnp.where(valid, dot(qs[h], ks[h], (1, 1)) * scale, -1e30) for h in heads]
+    grads = [dot(gs[h], vs[h], (1, 1)) for h in heads]
+    expos = [jnp.exp(s - jnp.max(s, axis=-1, keepdims=True)) for s in scores]
+    probs = [e * (1.0 / jnp.sum(e, axis=-1, keepdims=True)) for e in expos]
+    lows = [p.astype(BF) for p in probs]
+    outs = [dot(lows[h], vs[h], (1, 0)) for h in heads]
+    value_grads = [dot(lows[h], gs[h], (0, 0)) for h in heads]
+    deltas = [jnp.sum(gs[h].astype(F32) * outs[h], axis=-1, keepdims=True) for h in heads]
+    grads = [(probs[h] * (grads[h] - deltas[h])).astype(BF) for h in heads]
+    key_grads = [dot(grads[h], qs[h], (0, 0)) for h in heads]
+    query_grads = [dot(grads[h], ks[h], (1, 0)) for h in heads]
+    for h in heads:
+        sg[:, cols[h]] = (key_grads[h] * scale).astype(BF)
+        sg[:, vcols[h]] = value_grads[h].astype(BF)
+    for h in heads:
+        att[:, cols[h]] = outs[h].astype(BF)
+        qg[:, cols[h]] = (query_grads[h] * scale).astype(BF)
     stores = [
         pltpu.make_async_copy(att, att_hbm, load_sem.at[0]),
         pltpu.make_async_copy(qg, qg_hbm, load_sem.at[1]),
@@ -197,7 +206,7 @@
                 both = parts[half][:, 128 * c:128 * c + 128].reshape(4, 56, 128) + dpr[e, tile].astype(F32)
                 ha[tile, e], hb[e, tile] = both[:, :RA], both[:, RA:]
                 xsa[tile, e], zsb[e, tile] = both[:, :RA].astype(BF), both[:, RA:].astype(BF)
-        for s in range(1, NX):
+        for s in OTHERS:
             send(xsa.at[lax.rem(x + s, NX), e], xra.at[s - 1, e], 4, rxa_sem.at[e], along_x(s))
         to_class(
             lax.rem(e - ze + 4, 4), whole, first, second,
@@ -226,7 +235,7 @@
         total = add(hb[ze, tile], znb, tile)
         hbx[tile] = total
         xsb[tile] = total.astype(BF)
-    for s in range(1, NX):
+    for s in OTHERS:
         send(xsb.at[lax.rem(x + s, NX)], xrb.at[s - 1], 7, one_sem.at[2], along_x(s))
     fold_a(2)
     fold_a(3)
@@ -234,59 +243,77 @@
     total = add(hbx[x], xrb)
     ffb[...] = total
     fsb[...] = total.astype(BF)
-    for i in range(1, 4):
+    for i in OTHERS:
         send(fsb.at[lax.rem(zj + i, 4)], frb.at[i - 1], 9, one_sem.at[4], along_z(4 * i))
     wait_bytes(zna, one_sem.at[1])
     total = add(zfa[ze], zna)
     ffa[...] = total
     fsa[...] = total.astype(BF)
-    for i in range(1, 4):
+    for i in OTHERS:
         send(fsa.at[lax.rem(zj + i, 4)], fra.at[i - 1], 8, one_sem.at[3], along_z(4 * i))
     wait_bytes(frb, one_sem.at[4])
     gb[ze, x, zj] = add(ffb[zj], frb).astype(BF)
-    for i in range(1, 4):
+    for i in OTHERS:
         send(gb.at[ze, x, zj], gb.at[ze, x, zj], 11, one_sem.at[6], along_z(4 * i))
     wait_bytes(fra, one_sem.at[3])
     ga[x, ze, zj] = add(ffa[zj], fra).astype(BF)
-    for i in range(1, 4):
+    for i in OTHERS:
         send(ga.at[x, ze, zj], ga.at[x, ze, zj], 10, one_sem.at[5], along_z(4 * i))
 
     wait_bytes(frb, one_sem.at[6])
-    for s in range(1, NX):
+    for s in OTHERS:
         send(gb.at[ze, x], gb.at[ze, x], 14, one_sem.at[8], along_x(s))
     wait_bytes(fra, one_sem.at[5])
-    for i, (shift, some) in enumerate(((1, whole), (-1, whole), (2, first), (-2, second))):
-        send(ga.at[x, ze, some], ga.at[x, ze, some], 12, gna_sem.at[min(i, 2)], along_z(shift))
-    for s in range(1, NX):
+    for i, (shift, some) in enumerate(((2, first), (-2, second), (1, whole), (-1, whole))):
+        send(ga.at[x, ze, some], ga.at[x, ze, some], 12, gna_sem.at[max(i - 1, 0)], along_z(shift))
+    for s in OTHERS:
         send(ga.at[x, ze], ga.at[x, ze], 13, one_sem.at[7], along_x(s))
     wait_bytes(xrb, one_sem.at[8])
-    for shift, some in ((1, whole), (-1, whole), (2, first), (-2, second)):
+    for shift, some in ((2, first), (-2, second), (1, whole), (-1, whole)):
         send(gb.at[ze, some], gb.at[ze, some], 15, one_sem.at[9], along_z(shift))
-    for i, k in enumerate((3, 1, 2)):
+    for i, k in ((1, 3), (2, 1), (0, 2)):
         wait_bytes(zna.at[i], gna_sem.at[i])
         group = lax.rem(ze + k, 4)
-        for s in range(1, NX):
+        for s in OTHERS:
             send(ga.at[x, group], ga.at[x, group], 13, one_sem.at[7], along_x(s))
     wait_bytes(znb, one_sem.at[9])
     wait_bytes(xra, one_sem.at[7])
 
     for store in stores:
         store.wait()
-    wait_bytes(zbuf.at[pl.ds(1, 15)], send_sem.at[0])
-    wait_bytes(rows.at[:, pl.ds(1, 3), :, pl.ds(0, 256)], send_sem.at[1])
+    wait_bytes(held.at[pl.ds(1, 3)], send_sem.at[0])
+    wait_bytes(rows.at[:, pl.ds(1, NZ - 1), :, pl.ds(0, 256)], send_sem.at[1])
     wait_bytes(rows.at[:, :, :, pl.ds(0, 768)], send_sem.at[2])
     for phase, sized in enumerate((dps, xra, znb, zna, xrb, fra, frb, fra, frb, zna, xra, xrb, znb)):
         wait_bytes(sized, send_sem.at[phase + 3])
 
 
-def place(att_in, qg_in, ga, gb, att_out, qg_out, kg_out, vg_out):
-    att_out[...] = att_in[...]
-    qg_out[...] = qg_in[...]
-    for tile in range(4):
-        out = (kg_out, vg_out)[tile // 2]
-        lanes = pl.ds(128 * (tile % 2), 128)
-        out[:, :, pl.ds(0, RA), lanes] = ga[tile]
-        out[:, :, pl.ds(RA, RB), lanes] = gb[:, tile]
+def place(
+    att_in, qg_in, ga, gb, att_out, qg_out, kg_out, vg_out,
+    att, qg, ga_in, gb_in, kg, vg, in_sem, out_sem,
+):
+    pairs = [(att_in, att), (qg_in, qg)]
+    for half in range(2):
+        for tile in (2 * half, 2 * half + 1):
+            pairs += [(ga.at[tile], ga_in.at[tile]), (gb.at[:, tile], gb_in.at[tile])]
+    reads = [pltpu.make_async_copy(src, dst, in_sem.at[i]) for i, (src, dst) in enumerate(pairs)]
+    pairs = [(kg, kg_out), (vg, vg_out), (att, att_out), (qg, qg_out)]
+    writes = [pltpu.make_async_copy(src, dst, out_sem.at[i]) for i, (src, dst) in enumerate(pairs)]
+    for read in reads[2:] + reads[:2]:
+        read.start()
+    for half, out in enumerate((kg, vg)):
+        for read in reads[2 + 4 * half:6 + 4 * half]:
+            read.wait()
+        for c in range(2):
+            lanes = pl.ds(128 * c, 128)
+            out[:, :, pl.ds(0, RA), lanes] = ga_in[2 * half + c]
+            out[:, :, pl.ds(RA, RB), lanes] = gb_in[2 * half + c]
+        writes[half].start()
+    for i in range(2):
+        reads[i].wait()
+        writes[2 + i].start()
+    for write in writes:
+        write.wait()
 
 
 def body(queries, out_grad, encoded, key_weight, value_weight, neighbour_ids, neighbour_counts):
@@ -312,8 +339,8 @@
         out_specs=(hbm, hbm, vmem, vmem),
         scratch_shapes=[
             bf(1024, 1024), bf(128, 512), bf(128, 512), bf(128, 512), bf(128, 512),
-            bf(NZ, NX, 8, 256), bf(NZ, NX, 8, 256),
-            bf(NZ, NX, 8, 1024), bf(1024, 512), bf(512, 1024), bf(512, 1024),
+            bf(NX, NZ, 8, 256), bf(NX, NZ, 8, 256),
+            bf(NX, NZ, 8, 1024), bf(1024, 512), bf(512, 1024), bf(512, 1024),
             bf(4, 4, 4, 56, 128), bf(4, 4, 4, 56, 128),
             f32(4, 4, 4, RA, 128), f32(4, 4, 4, RB, 128),
             bf(4, 4, 4, RA, 128), bf(4, 4, 4, RB, 128),
@@ -337,8 +364,13 @@
     att, qg, kg, vg = pl.pallas_call(
         place,
         out_shape=(low, low, grad, grad),
-        in_specs=[vmem] * 4,
-        out_specs=(vmem,) * 4,
+        in_specs=[hbm] * 4,
+        out_specs=(hbm,) * 4,
+        scratch_shapes=[
+            bf(128, 512), bf(128, 512), bf(4, 4, 4, RA, 128), bf(4, 4, 4, RB, 128),
+            bf(4, 4, 56, 256), bf(4, 4, 56, 256), dma((10,)), dma((4,)),
+        ],
+        compiler_params=pltpu.CompilerParams(vmem_limit_bytes=56 * 1024 * 1024),
     )(att, qg, ga, gb)
     return (
         att.reshape(1, 2, 64, 512), qg.reshape(1, 2, 64, 512),

time: 86.9 us -> 82.5 us (0.949)
  the two profiles are of different devices: /device:TPU:32 before, /device:TPU:2 now
where the time goes in v3:
time: 82.5 us; the launch traced here: 82.4 us
  Pallas kernels  81.7 us (99%)
    pallas_call x1, Pallas kernels, body(): pl.pallas_call(kernel, out_shape=(low, low, jax.ShapeDtypeStruct((4, 4, 4...  79.4 us
    pallas_call x1, Pallas kernels, body(): pl.pallas_call(place, out_shape=(low, low, grad, grad), in_specs=[hbm] *...  2.3 us

profile of v3, /device:TPU:2, one launch (start us, length us, event | category | flops | bytes accessed | tf_op | source)
XLA Modules:
  0.0 82.4 jit_solution(15800269100065778872)
XLA Ops:
  0.6 79.4 %shard_map.102 = (bf16[128,512]{1,0:T(8,128)(2,1)}, bf16[128,512]{1,0:T(8,128)(2,1)}, bf16[4,4,4,32,128]{4,3,2,1,0:T(8,128)(2,1)}, bf16[4,4,4,24,128]{4,3,2,1,0:T(8,128)(2,1)}) custom-call(s32[2,128]{1,0:T(2,128)} %bitcast.19, s32[1,2]{1,0:T(1,128)} %counts_ref.1, bf16[2,224,256]{2,1,0:T(8,128)(2,1)} %bitcast.14, bf16[128,512]{1,0:T(8,128)(2,1)} %bitcast.15, ...), custom_call_target="tpu_custom_call" | custom-call | flops 2500000000 | bytes 4000000 | tf_op jit(solution)/shard_map/pallas_call | solution.py:331
  80.1 2.3 %shard_map.103 = (bf16[128,512]{1,0:T(8,128)(2,1)}, bf16[128,512]{1,0:T(8,128)(2,1)}, bf16[4,4,56,256]{3,2,1,0:T(8,128)(2,1)}, bf16[4,4,56,256]{3,2,1,0:T(8,128)(2,1)}) custom-call(bf16[128,512]{1,0:T(8,128)(2,1)} %get-tuple-element.12.att_in, bf16[128,512]{1,0:T(8,128)(2,1)} %get-tuple-element.13.qg_in, bf16[4,4,4,32,128]{4,3,2,1,0:T(8,128)(2,1)} %get-tuple-element.14.ga, ...), custom_call_target="tpu_custom_call" | custom-call | tf_op jit(solution)/shard_map/pallas_call | solution.py:364

commit v4 on v3

--- a/solution.py
+++ b/solution.py
@@ -14,6 +14,7 @@
 F32 = jnp.float32
 SHIFT = (0, 8, 7, 9, 6, 10, 5, 11, 4, 12, 3, 13, 2, 14, 1, 15)
 OTHERS = (2, 1, 3)
+RUNS = ((0, 6), (6, 11), (11, 16))
 
 
 def dot(a, b, dims):
@@ -32,8 +33,8 @@
     ids_ref, counts_ref, enc_ref, q_hbm, og_hbm, wk_hbm, wv_hbm,
     att_hbm, qg_hbm, ga, gb,
     w, q, og, att, qg, outgoing, held, rows, rows_t, kv, sg, dps, dpr,
-    ha, hb, xsa, zsb, xra, znb, zfa, zsa, zna, hbx, xsb, xrb, ffa, fsa, fra, ffb, fsb, frb,
-    load_sem, send_sem, ax_sem, az_sem, ay_sem, dp_sem, rxa_sem, one_sem, gna_sem,
+    ha, hb, xsa, zsb, xra, znb, zfa, zsa, zna, hbx, xsb, xrb, ffa, fsa, fra, gar, ffb, fsb, frb,
+    load_sem, send_sem, ax_sem, az_sem, ay_sem, dp_sem, rxa_sem, one_sem, gza_sem,
 ):
     seq = lax.axis_index("seq")
     m = lax.axis_index("mp")
@@ -158,19 +159,9 @@
     deltas = [jnp.sum(gs[h].astype(F32) * outs[h], axis=-1, keepdims=True) for h in heads]
     grads = [(probs[h] * (grads[h] - deltas[h])).astype(BF) for h in heads]
     key_grads = [dot(grads[h], qs[h], (0, 0)) for h in heads]
-    query_grads = [dot(grads[h], ks[h], (1, 0)) for h in heads]
     for h in heads:
         sg[:, cols[h]] = (key_grads[h] * scale).astype(BF)
         sg[:, vcols[h]] = value_grads[h].astype(BF)
-    for h in heads:
-        att[:, cols[h]] = outs[h].astype(BF)
-        qg[:, cols[h]] = (query_grads[h] * scale).astype(BF)
-    stores = [
-        pltpu.make_async_copy(att, att_hbm, load_sem.at[0]),
-        pltpu.make_async_copy(qg, qg_hbm, load_sem.at[1]),
-    ]
-    for store in stores:
-        store.start()
 
     def partial(e, side, half):
         cols = pl.ds(pl.multiple_of(512 * half + 256 * side, 256), 256)
@@ -197,6 +188,15 @@
             for c in range(2):
                 dps[e, 2 * half + c] = part[:, 128 * c:128 * c + 128].reshape(4, 56, 128).astype(BF)
         send(dps.at[e], dpr.at[e], 3, dp_sem.at[e], sibling)
+    for h in heads:
+        att[:, cols[h]] = outs[h].astype(BF)
+        qg[:, cols[h]] = (dot(grads[h], ks[h], (1, 0)) * scale).astype(BF)
+    stores = [
+        pltpu.make_async_copy(att, att_hbm, load_sem.at[0]),
+        pltpu.make_async_copy(qg, qg_hbm, load_sem.at[1]),
+    ]
+    for store in stores:
+        store.start()
     for e in range(4):
         parts = [partial(e, d, half) for half in range(2)]
         wait_bytes(dpr.at[e], dp_sem.at[e])
@@ -256,36 +256,51 @@
     for i in OTHERS:
         send(gb.at[ze, x, zj], gb.at[ze, x, zj], 11, one_sem.at[6], along_z(4 * i))
     wait_bytes(fra, one_sem.at[3])
-    ga[x, ze, zj] = add(ffa[zj], fra).astype(BF)
-    for i in OTHERS:
-        send(ga.at[x, ze, zj], ga.at[x, ze, zj], 10, one_sem.at[5], along_z(4 * i))
+    gar[x, 0] = add(ffa[zj], fra).astype(BF)
+    run_of = [run for run, (low, high) in enumerate(RUNS) for _ in range(low, high)]
+    for p in range(1, NZ):
+        send(gar.at[x, 0], gar.at[x, p], 10, gza_sem.at[run_of[p]], along_z(SHIFT[p]))
+
+    def spread(run):
+        low, high = RUNS[run]
+        wait_bytes(gar.at[0, pl.ds(max(low, 1), high - max(low, 1))], gza_sem.at[run])
+        for s in OTHERS:
+            some = gar.at[x, pl.ds(low, high - low)]
+            send(some, some, 13, one_sem.at[7], along_x(s))
 
     wait_bytes(frb, one_sem.at[6])
     for s in OTHERS:
         send(gb.at[ze, x], gb.at[ze, x], 14, one_sem.at[8], along_x(s))
-    wait_bytes(fra, one_sem.at[5])
-    for i, (shift, some) in enumerate(((2, first), (-2, second), (1, whole), (-1, whole))):
-        send(ga.at[x, ze, some], ga.at[x, ze, some], 12, gna_sem.at[max(i - 1, 0)], along_z(shift))
-    for s in OTHERS:
-        send(ga.at[x, ze], ga.at[x, ze], 13, one_sem.at[7], along_x(s))
+
+    def tile_to_z(back):
+        tile = gb.at[ze, lax.rem(x + NX - back, NX)]
+        for shift in (2 if back % 2 == 0 else -2, 1, -1):
+            send(tile, tile, 15, one_sem.at[9], along_z(shift))
+
+    tile_to_z(0)
+    spread(0)
     wait_bytes(xrb, one_sem.at[8])
-    for shift, some in ((2, first), (-2, second), (1, whole), (-1, whole)):
-        send(gb.at[ze, some], gb.at[ze, some], 15, one_sem.at[9], along_z(shift))
-    for i, k in ((1, 3), (2, 1), (0, 2)):
-        wait_bytes(zna.at[i], gna_sem.at[i])
-        group = lax.rem(ze + k, 4)
-        for s in OTHERS:
-            send(ga.at[x, group], ga.at[x, group], 13, one_sem.at[7], along_x(s))
+    for back in range(1, NX):
+        tile_to_z(back)
+    spread(1)
+    spread(2)
+    wait_bytes(gar.at[pl.ds(0, 3)], one_sem.at[7])
+    for p in range(NZ):
+        origin = lax.rem(z + NZ - SHIFT[p], NZ)
+        ga[:, lax.rem(origin, 4), origin // 4] = gar[:, p]
     wait_bytes(znb, one_sem.at[9])
-    wait_bytes(xra, one_sem.at[7])
 
     for store in stores:
         store.wait()
     wait_bytes(held.at[pl.ds(1, 3)], send_sem.at[0])
     wait_bytes(rows.at[:, pl.ds(1, NZ - 1), :, pl.ds(0, 256)], send_sem.at[1])
     wait_bytes(rows.at[:, :, :, pl.ds(0, 768)], send_sem.at[2])
-    for phase, sized in enumerate((dps, xra, znb, zna, xrb, fra, frb, fra, frb, zna, xra, xrb, znb)):
-        wait_bytes(sized, send_sem.at[phase + 3])
+    sent = (
+        (3, dps), (4, xra), (5, znb), (6, zna), (7, xrb), (8, fra), (9, frb), (10, gar.at[0, pl.ds(1, 15)]),
+        (11, frb), (13, gar.at[pl.ds(0, 3)]), (14, xrb), (15, znb),
+    )
+    for phase, sized in sent:
+        wait_bytes(sized, send_sem.at[phase])
 
 
 def place(
@@ -348,6 +363,7 @@
             f32(4, 4, RA, 128), bf(4, 4, RA, 128), bf(3, 4, RA, 128),
             f32(4, 4, RB, 128), bf(4, 4, RB, 128), bf(3, 4, RB, 128),
             f32(4, RA, 128), bf(4, RA, 128), bf(3, RA, 128),
+            bf(4, NZ, RA, 128),
             f32(4, RB, 128), bf(4, RB, 128), bf(3, RB, 128),
             dma((10,)), dma((16,)), dma((4,)), dma((4,)), dma((4,)),
             dma((4,)), dma((4,)), dma((10,)), dma((3,)),

time: 82.5 us -> 81.5 us (0.988)
  the two profiles are of different devices: /device:TPU:2 before, /device:TPU:32 now
where the time goes in v4:
time: 81.5 us; the launch traced here: 81.3 us
  Pallas kernels  80.7 us (99%)
    pallas_call x1, Pallas kernels, body(): pl.pallas_call(kernel, out_shape=(low, low, jax.ShapeDtypeStruct((4, 4, 4...  78.4 us
    pallas_call x1, Pallas kernels, body(): pl.pallas_call(place, out_shape=(low, low, grad, grad), in_specs=[hbm] *...  2.3 us

profile of v4, /device:TPU:32, one launch (start us, length us, event | category | flops | bytes accessed | tf_op | source)
XLA Modules:
  0.0 81.3 jit_solution(4207231322402434447)
XLA Ops:
  0.6 78.4 %shard_map.102 = (bf16[128,512]{1,0:T(8,128)(2,1)}, bf16[128,512]{1,0:T(8,128)(2,1)}, bf16[4,4,4,32,128]{4,3,2,1,0:T(8,128)(2,1)}, bf16[4,4,4,24,128]{4,3,2,1,0:T(8,128)(2,1)}) custom-call(s32[2,128]{1,0:T(2,128)} %bitcast.19, s32[1,2]{1,0:T(1,128)} %counts_ref.1, bf16[2,224,256]{2,1,0:T(8,128)(2,1)} %bitcast.14, bf16[128,512]{1,0:T(8,128)(2,1)} %bitcast.15, ...), custom_call_target="tpu_custom_call" | custom-call | flops 2500000000 | bytes 4000000 | tf_op jit(solution)/shard_map/pallas_call | solution.py:346
  79.0 2.3 %shard_map.103 = (bf16[128,512]{1,0:T(8,128)(2,1)}, bf16[128,512]{1,0:T(8,128)(2,1)}, bf16[4,4,56,256]{3,2,1,0:T(8,128)(2,1)}, bf16[4,4,56,256]{3,2,1,0:T(8,128)(2,1)}) custom-call(bf16[128,512]{1,0:T(8,128)(2,1)} %get-tuple-element.12.att_in, bf16[128,512]{1,0:T(8,128)(2,1)} %get-tuple-element.13.qg_in, bf16[4,4,4,32,128]{4,3,2,1,0:T(8,128)(2,1)} %get-tuple-element.14.ga, ...), custom_call_target="tpu_custom_call" | custom-call | tf_op jit(solution)/shard_map/pallas_call | solution.py:380

commit v5 on v4

--- a/solution.py
+++ b/solution.py
@@ -14,7 +14,7 @@
 F32 = jnp.float32
 SHIFT = (0, 8, 7, 9, 6, 10, 5, 11, 4, 12, 3, 13, 2, 14, 1, 15)
 OTHERS = (2, 1, 3)
-RUNS = ((0, 6), (6, 11), (11, 16))
+RUNS = ((0, 6), (6, 10), (10, 13), (13, 16))
 
 
 def dot(a, b, dims):
@@ -282,8 +282,8 @@
     wait_bytes(xrb, one_sem.at[8])
     for back in range(1, NX):
         tile_to_z(back)
-    spread(1)
-    spread(2)
+    for run in range(1, len(RUNS)):
+        spread(run)
     wait_bytes(gar.at[pl.ds(0, 3)], one_sem.at[7])
     for p in range(NZ):
         origin = lax.rem(z + NZ - SHIFT[p], NZ)
@@ -366,7 +366,7 @@
             bf(4, NZ, RA, 128),
             f32(4, RB, 128), bf(4, RB, 128), bf(3, RB, 128),
             dma((10,)), dma((16,)), dma((4,)), dma((4,)), dma((4,)),
-            dma((4,)), dma((4,)), dma((10,)), dma((3,)),
+            dma((4,)), dma((4,)), dma((10,)), dma((len(RUNS),)),
         ],
         compiler_params=pltpu.CompilerParams(
             collective_id=0, has_side_effects=True, vmem_limit_bytes=56 * 1024 * 1024

time: 81.5 us -> 81.7 us (level)
  no operation moved by 1% of the time
where the time goes in v5:
time: 81.7 us; the launch traced here: 81.5 us
  Pallas kernels  80.9 us (99%)
    pallas_call x1, Pallas kernels, body(): pl.pallas_call(kernel, out_shape=(low, low, jax.ShapeDtypeStruct((4, 4, 4...  78.6 us
    pallas_call x1, Pallas kernels, body(): pl.pallas_call(place, out_shape=(low, low, grad, grad), in_specs=[hbm] *...  2.3 us

profile of v5, /device:TPU:32, one launch (start us, length us, event | category | flops | bytes accessed | tf_op | source)
XLA Modules:
  0.0 81.5 jit_solution(15434276307814036912)
XLA Ops:
  0.6 78.6 %shard_map.102 = (bf16[128,512]{1,0:T(8,128)(2,1)}, bf16[128,512]{1,0:T(8,128)(2,1)}, bf16[4,4,4,32,128]{4,3,2,1,0:T(8,128)(2,1)}, bf16[4,4,4,24,128]{4,3,2,1,0:T(8,128)(2,1)}) custom-call(s32[2,128]{1,0:T(2,128)} %bitcast.19, s32[1,2]{1,0:T(1,128)} %counts_ref.1, bf16[2,224,256]{2,1,0:T(8,128)(2,1)} %bitcast.14, bf16[128,512]{1,0:T(8,128)(2,1)} %bitcast.15, ...), custom_call_target="tpu_custom_call" | custom-call | flops 2500000000 | bytes 4000000 | tf_op jit(solution)/shard_map/pallas_call | solution.py:346
  79.2 2.3 %shard_map.103 = (bf16[128,512]{1,0:T(8,128)(2,1)}, bf16[128,512]{1,0:T(8,128)(2,1)}, bf16[4,4,56,256]{3,2,1,0:T(8,128)(2,1)}, bf16[4,4,56,256]{3,2,1,0:T(8,128)(2,1)}) custom-call(bf16[128,512]{1,0:T(8,128)(2,1)} %get-tuple-element.12.att_in, bf16[128,512]{1,0:T(8,128)(2,1)} %get-tuple-element.13.qg_in, bf16[4,4,4,32,128]{4,3,2,1,0:T(8,128)(2,1)} %get-tuple-element.14.ga, ...), custom_call_target="tpu_custom_call" | custom-call | tf_op jit(solution)/shard_map/pallas_call | solution.py:380
